TPU v7x, 512 devices: a whole 4x4x16 slice. The times are simulated.
512 devices in a mesh: req: 128 (over z, y_lo, x), tp: 4 (over y_hi, core).
Axes of the slice: x: 4, y: 4 (y_hi: 2, y_lo: 2; y = y_hi * 2 + y_lo), z: 16, core: 2. Of those that a mesh axis runs over, the one named last changes fastest.
Arguments:
- hidden: bfloat16 [8192, 2048], P('req'), may hold values from -6 to 6
- draft_query: bfloat16 [8192, 2048], P('req', 'tp'), may hold values from -180 to 180
- draft_kv: bfloat16 [2, 8192, 2048], P(None, 'req', 'tp'), may hold values from -6 to 6
- cache_kv: bfloat16 [2, 32768, 2048], P(None, 'req', 'tp'), may hold values from -6 to 6
- piece_offset: int32 [256], P('req'), may hold values from 0 to 3
- piece_length: int32 [256], P('req'), may hold values from 1 to 128
- ancestors: int32 [8192, 64], P('req'), may hold values from 0 to 1, as said below
- out_proj: bfloat16 [2048, 2048], P('tp'), may hold values from -0.125 to 0.125
- ffn_gain: float32 [2048], replicated, may hold values from 0.1 to 1.9
- router_w: bfloat16 [2048, 64], replicated, may hold values from -0.125 to 0.125
- expert_gate_up: bfloat16 [2, 2048, 65536], P(None, None, ('req', 'tp')), may hold values from -0.125 to 0.125
- expert_down: bfloat16 [65536, 2048], P(('req', 'tp')), may hold values from -1.5 to 1.5
- expert_ids: int32 [8192, 8], P('req'), may hold values from 0 to 63, all different within a row; in each aligned block of 64 rows (0 to 63, 64 to 127, ...) at most 12 rows name the same one
- accepted_ids: int32 [1024], P('req'), may hold values from 0 to 63
Outputs:
- layer_out: bfloat16 [8192, 2048], P('req', 'tp')
- attended: bfloat16 [8192, 2048], P('req', 'tp')
- accepted_kv: bfloat16 [2, 1024, 2048], P(None, 'req', 'tp')
Inputs may be any that keep to these rules, and one draw needn't show every extreme that they name: Piece p of device d belongs to the request of device (d - piece_offset[p]) mod 128. Within each request's 64 rows, row i marks node i and all its ancestors; node 0 is the root and every other node's parent has a lower number. `expert_ids`: each row names 8 different experts; in the rows of one device no expert is named by more than 12 rows, a bound that some block reaches.
All inputs are finite; a program needn't handle non-finite values.
Results may differ from a plain program's by a relative error of at most 0.03.
Values may be sent and summed in bfloat16 or wider, within the bound.
A program may use at most 64 MiB of HBM per device.

v0:
```python
import jax
import jax.numpy as jnp
from jax import lax
from jax.sharding import PartitionSpec as P

HD = 128
PIECES = 2
PIECE = 128
SPAN = 4
NEG = -1e30


def passed_along(value, axis, by):
    devices = lax.axis_size(axis)
    return lax.ppermute(value, axis, [(i, (i + by) % devices) for i in range(devices)])


def partials(scores, mask, values, equation):
    top = jnp.max(jnp.where(mask, scores, NEG), axis=-1)
    weights = jnp.where(mask, jnp.exp(scores - top[..., None]), 0.0)
    total = jnp.sum(weights, axis=-1)
    acc = jnp.einsum(
        equation, weights.astype(jnp.bfloat16), values, preferred_element_type=jnp.float32
    )
    return (top, total, acc)


def finish_expert(gate, upper, expert_down, shape):
    act = (jax.nn.silu(gate) * upper).astype(jnp.bfloat16)
    result = (
        jnp.dot(act, expert_down, preferred_element_type=jnp.float32)
        .astype(jnp.bfloat16)
        .reshape(shape)
    )
    return lax.all_to_all(result, "req", split_axis=0, concat_axis=0, tiled=True)


def body(
    hidden,
    draft_query,
    draft_kv,
    cache_kv,
    piece_offset,
    piece_length,
    ancestors,
    out_proj,
    ffn_gain,
    router_w,
    expert_gate_up,
    expert_down,
    expert_ids,
    accepted_ids,
):
    rows = hidden.shape[0]
    local_heads = draft_query.shape[1] // HD
    scale = HD ** (-0.5)
    query = draft_query.reshape(rows, local_heads, HD)
    own_keys = draft_kv[0].reshape(rows, local_heads, HD)
    own_values = draft_kv[1].reshape(rows, local_heads, HD)
    pieces = cache_kv.reshape(2, PIECES, PIECE, local_heads, HD)
    slots = jnp.arange(PIECE, dtype=jnp.int32)
    dscores = (
        jnp.einsum("thd,shd->ths", query, own_keys, preferred_element_type=jnp.float32) * scale
    )
    dtop, dtotal, dacc = partials(dscores, (ancestors > 0)[:, None, :], own_values, "ths,shd->thd")
    parts = [(dtop[None], dtotal[None], dacc[None])]
    tags = jnp.stack([piece_offset, piece_length]).astype(jnp.bfloat16)
    for step in range(SPAN):
        if step == 0:
            kv_here, tag_here = (pieces, tags)
        else:
            kv_here, tag_here = passed_along((pieces, tags), "req", -step)
        valid = (tag_here[0] == step)[:, None] & (
            slots[None, :].astype(jnp.float32) < tag_here[1].astype(jnp.float32)[:, None]
        )
        scores = (
            jnp.einsum("thd,pshd->pths", query, kv_here[0], preferred_element_type=jnp.float32)
            * scale
        )
        parts.append(partials(scores, valid[:, None, None, :], kv_here[1], "pths,pshd->pthd"))
    tops = jnp.concatenate([item[0] for item in parts])
    totals = jnp.concatenate([item[1] for item in parts])
    accs = jnp.concatenate([item[2] for item in parts])
    best = jnp.max(tops, axis=0)
    factor = jnp.exp(tops - best[None])
    merged = jnp.sum(factor[..., None] * accs, axis=0) / jnp.sum(factor * totals, axis=0)[..., None]
    attended = merged.astype(jnp.bfloat16).reshape(rows, local_heads * HD)
    partial_proj = jnp.dot(attended, out_proj, preferred_element_type=jnp.float32)
    attn_proj = lax.psum(partial_proj.astype(jnp.bfloat16), "tp").astype(jnp.float32)
    residual = (hidden.astype(jnp.float32) + attn_proj).astype(jnp.bfloat16)
    resf = residual.astype(jnp.float32)
    normed = (
        resf * lax.rsqrt(jnp.mean(resf * resf, axis=1, keepdims=True) + 1e-06) * ffn_gain
    ).astype(jnp.bfloat16)
    logits = jnp.dot(normed, router_w, preferred_element_type=jnp.float32)
    experts = router_w.shape[1]
    top_count = expert_ids.shape[1]
    picks = expert_ids[:, :, None] == jnp.arange(experts, dtype=jnp.int32)
    chosen = jnp.sum(jnp.where(picks, logits[:, None, :], 0.0), axis=2)
    gates = jax.nn.softmax(chosen, axis=1).astype(jnp.bfloat16)
    routed = jnp.sum(picks.astype(jnp.int32), axis=1)
    gate_of = jnp.sum(jnp.where(picks, gates.astype(jnp.float32)[:, :, None], 0.0), axis=1)
    capacity = min(rows, 3 * ((rows * top_count + experts - 1) // experts) // 2)
    rank = jnp.cumsum(routed, axis=0) - routed
    placed = (routed[:, :, None] > 0) & (rank[:, :, None] == jnp.arange(capacity, dtype=jnp.int32))
    outgoing = jnp.einsum(
        "tec,tm->ecm", placed.astype(jnp.bfloat16), normed, preferred_element_type=jnp.float32
    ).astype(jnp.bfloat16)
    outgoing = jnp.repeat(outgoing, 2, axis=0)
    received = lax.all_to_all(outgoing, "req", split_axis=0, concat_axis=0, tiled=True)
    flat = received.reshape(-1, received.shape[2])
    gate = jnp.dot(flat, expert_gate_up[0], preferred_element_type=jnp.float32)
    upper = jnp.dot(flat, expert_gate_up[1], preferred_element_type=jnp.float32)
    returned = finish_expert(gate, upper, expert_down, received.shape)
    weighting = jnp.repeat(
        (placed.astype(jnp.float32) * gate_of[:, :, None]).astype(jnp.bfloat16), 2, axis=1
    )
    moe_part = jnp.einsum("tdc,dcm->tm", weighting, returned, preferred_element_type=jnp.float32)
    moe = lax.psum_scatter(
        moe_part.astype(jnp.bfloat16), "tp", scatter_dimension=1, tiled=True
    ).astype(jnp.float32)
    cols = moe.shape[1]
    residual_part = lax.dynamic_slice_in_dim(resf, lax.axis_index("tp") * cols, cols, 1)
    layer_out = (residual_part + moe).astype(jnp.bfloat16)
    accepted_kv = jnp.take(draft_kv, accepted_ids, axis=1)
    return (layer_out, attended, accepted_kv)


def solution(mesh):
    in_specs = (
        P("req", None),
        P("req", "tp"),
        P(None, "req", "tp"),
        P(None, "req", "tp"),
        P("req"),
        P("req"),
        P("req", None),
        P("tp", None),
        P(),
        P(),
        P(None, None, ("req", "tp")),
        P(("req", "tp"), None),
        P("req", None),
        P("req"),
    )
    out_specs = (P("req", "tp"), P("req", "tp"), P(None, "req", "tp"))
    return jax.shard_map(body, mesh=mesh, in_specs=in_specs, out_specs=out_specs, check_vma=False)
```

profile of v0, /device:TPU:1, one launch (start us, length us, event | category | flops | bytes accessed | tf_op | source)
XLA Modules:
  0.0 1011.8 jit_solution(13778763631182478897)
XLA Ops:
  9.3 13.9 %collective-permute-start.4 = (bf16[2,2]{1,0:T(2,128)(2,1)}, bf16[2,2]{1,0:T(2,128)(2,1)}, u32[]{:S(2)}, u32[]{:S(2)}) collective-permute-start(bf16[2,2]{1,0:T(2,128)(2,1)} %pad_maximum_fusion), channel_id=1, source_target_pairs={{0,500},{4,504},{8,508},{12,0},{16,4},{20,8},{24,12},{28,16},{32,2... | collective-permute-start | bytes 32 | tf_op jit(solution)/shard_map/ppermute | solution.py:15
  23.1 4.2 collective-permute-start.2
  27.4 3.1 collective-permute-start
  32.6 1.9 collective-permute-start.1
  34.5 4.8 collective-permute-start.5
  40.5 1.8 fusion.77
  46.6 2.5 collective-permute-start.3
  53.7 1.9 select_reduce_fusion.9
  55.6 3.2 collective-permute-done.5
  60.1 1.4 fusion.47
  61.5 8.5 collective-permute-done.3
  71.2 1.4 fusion.45
  72.7 2.5 select_reduce_fusion.7
  75.2 2.7 concatenate.16
  77.9 2.6 fusion.41
  81.2 2.7 concatenate.18
  85.8 1.3 fusion.11
  92.5 54.9 %all-reduce.2.cloned.1.call-done = bf16[64,2048]{1,0:T(8,128)(2,1)} async-done(((bf16[64,2048]{1,0:T(8,128)(2,1)}), bf16[64,2048]{1,0:T(8,128)(2,1)}) %all-reduce.2.cloned.1.call-update) | async-done | bytes 262160 | tf_op jit(solution)/shard_map/psum | solution.py:89
  147.4 1.9 fusion.34
  149.3 2.0 convolution_convert_fusion.1
  151.3 1.8 copy.187
  153.1 4.3 broadcast_in_dim.165
  157.4 380.0 %all_to_all.10 = bf16[128,12,2048]{2,1,0:T(8,128)(2,1)} all-to-all(bf16[128,12,2048]{2,1,0:T(8,128)(2,1)} %bitcast.127), channel_id=1, replica_groups=mesh['req'=128,'tp'=4] {'req'}, dimensions={0} | all-to-all | bytes 12582912 | tf_op jit(solution)/shard_map/all_to_all | solution.py:110
  537.4 10.8 %reshape.367 = bf16[1536,2048]{1,0:T(8,128)(2,1)} reshape(bf16[128,12,2048]{2,1,0:T(8,128)(2,1)} %all_to_all.10) | data formatting | bytes 12582912 | tf_op jit(solution)/shard_map/reshape | solution.py:111
  548.2 4.6 fusion.26
  552.8 11.9 %convolution_convert_fusion = bf16[1536,2048]{1,0:T(8,128)(2,1)} fusion(bf16[128,2048]{1,0:T(8,128)(2,1)S(1)} %copy-done.4, bf16[1536,2048]{1,0:T(8,128)(2,1)} %reshape.367, f32[1536,128]{1,0:T(8,128)S(1)} %fusion.26, bf16[2,2048,128]{2,1,0:T(8,128)(2,1)S(1)} %copy-done.8), kind=kOutput, calls=%fused_computation.1 | convolution fusion | flops 1614938112 | bytes 14417920 | tf_op jit(solution)/shard_map/dot_general | solution.py:31
  564.7 10.6 %reshape.368 = bf16[128,12,2048]{2,1,0:T(8,128)(2,1)} reshape(bf16[1536,2048]{1,0:T(8,128)(2,1)} %convolution_convert_fusion) | data formatting | bytes 12582912 | tf_op jit(solution)/shard_map/reshape | solution.py:33
  575.3 14.2 %all-to-all-start.1 = ((bf16[128,12,2048]{2,1,0:T(8,128)(2,1)}), bf16[128,12,2048]{2,1,0:T(8,128)(2,1)}, u32[]{:S(2)}, u32[]{:S(2)}) async-start(bf16[128,12,2048]{2,1,0:T(8,128)(2,1)} %reshape.368), calls=%async_computation.1 | async-start | bytes 16777216 | tf_op jit(solution)/shard_map/all_to_all | solution.py:35
  591.1 358.5 %all-to-all-done.1 = bf16[128,12,2048]{2,1,0:T(8,128)(2,1)} async-done(((bf16[128,12,2048]{2,1,0:T(8,128)(2,1)}), bf16[128,12,2048]{2,1,0:T(8,128)(2,1)}, u32[]{:S(2)}, u32[]{:S(2)}) %all-to-all-start.1) | async-done | bytes 6291488 | tf_op jit(solution)/shard_map/all_to_all | solution.py:35
  950.0 11.2 %fusion.6 = bf16[64,2048]{1,0:T(8,128)(2,1)} fusion(bf16[64,128,12]{0,1,2:T(8,128)(2,1)S(1)} %bitcast.128, bf16[128,12,2048]{2,1,0:T(8,128)(2,1)} %all-to-all-done.1), kind=kOutput, calls=%fused_computation.8 | convolution fusion | flops 402784256 | bytes 6750208 | tf_op jit(solution)/shard_map/tdc,dcm->tm/dot_general | solution.py:118
  962.5 40.9 %reduce-scatter.2.cloned.1.call-done = bf16[64,512]{1,0:T(8,128)(2,1)} async-done(((bf16[64,2048]{1,0:T(8,128)(2,1)}), bf16[64,512]{1,0:T(8,128)(2,1)}) %reduce-scatter.2.cloned.1.call-update) | async-done | bytes 65552 | tf_op jit(solution)/shard_map/reduce_scatter | solution.py:119
  1003.4 1.6 add_convert_fusion.1
  (110 shorter events, 27.6 us)
Async XLA Ops:
  7.2 82.9 %copy-start = (bf16[512,2048]{1,0:T(8,128)(2,1)S(1)}, bf16[512,2048]{1,0:T(8,128)(2,1)}, u32[]{:S(2)}) copy-start(bf16[512,2048]{1,0:T(8,128)(2,1)} %param.21) | copy-start | bytes 6291460
  7.2 35.1 %copy-start.11 = (bf16[64,512]{1,0:T(8,128)(2,1)S(1)}, bf16[64,512]{1,0:T(8,128)(2,1)}, u32[]{:S(2)}) copy-start(bf16[64,512]{1,0:T(8,128)(2,1)} %param.15) | copy-start | bytes 196612
  7.2 36.5 %copy-start.12 = (s32[64,64]{1,0:T(8,128)S(1)}, s32[64,64]{1,0:T(8,128)}, u32[]{:S(2)}) copy-start(s32[64,64]{1,0:T(8,128)} %param.20) | copy-start | bytes 49156
  7.2 36.6 %copy-start.6 = (bf16[2,64,512]{2,1,0:T(8,128)(2,1)S(1)}, bf16[2,64,512]{2,1,0:T(8,128)(2,1)}, u32[]{:S(2)}) copy-start(bf16[2,64,512]{2,1,0:T(8,128)(2,1)} %param.16) | copy-start | bytes 393220
  7.2 38.7 %copy-start.16 = (s32[64,8]{0,1:T(8,128)S(1)}, s32[64,8]{0,1:T(8,128)}, u32[]{:S(2)}) copy-start(s32[64,8]{0,1:T(8,128)} %param.26) | copy-start | bytes 6148
  7.2 140.2 %all-reduce.2.cloned.1.call-start = ((), (), s32[]{:S(2)}) async-start(), calls=%async_computation.3 | async-start | bytes 524288 | tf_op jit(solution)/shard_map/psum | solution.py:89
  9.3 37.4 %collective-permute-start.4 = (bf16[2,2]{1,0:T(2,128)(2,1)}, bf16[2,2]{1,0:T(2,128)(2,1)}, u32[]{:S(2)}, u32[]{:S(2)}) collective-permute-start(bf16[2,2]{1,0:T(2,128)(2,1)} %pad_maximum_fusion), channel_id=1, source_target_pairs={{0,500},{4,504},{8,508},{12,0},{16,4},{20,8},{24,12},{28,16},{32,2... | collective-permute-start | bytes 32 | tf_op jit(solution)/shard_map/ppermute | solution.py:15
  23.1 27.3 %collective-permute-start.2 = (bf16[2,2]{1,0:T(2,128)(2,1)}, bf16[2,2]{1,0:T(2,128)(2,1)}, u32[]{:S(2)}, u32[]{:S(2)}) collective-permute-start(bf16[2,2]{1,0:T(2,128)(2,1)} %pad_maximum_fusion), channel_id=1, source_target_pairs={{0,504},{4,508},{8,0},{12,4},{16,8},{20,12},{24,16},{28,20},{32,24... | collective-permute-start | bytes 32 | tf_op jit(solution)/shard_map/ppermute | solution.py:15
  27.4 24.3 %collective-permute-start = (bf16[2,2]{1,0:T(2,128)(2,1)}, bf16[2,2]{1,0:T(2,128)(2,1)}, u32[]{:S(2)}, u32[]{:S(2)}) collective-permute-start(bf16[2,2]{1,0:T(2,128)(2,1)} %pad_maximum_fusion), channel_id=1, source_target_pairs={{0,508},{4,0},{8,4},{12,8},{16,12},{20,16},{24,20},{28,24},{32,28}... | collective-permute-start | bytes 32 | tf_op jit(solution)/shard_map/ppermute | solution.py:15
  32.6 40.1 %collective-permute-start.1 = (bf16[2,2,128,4,128]{4,2,1,3,0:T(8,128)(2,1)}, bf16[2,2,128,4,128]{4,2,1,3,0:T(8,128)(2,1)}, u32[]{:S(2)}, u32[]{:S(2)}) collective-permute-start(bf16[2,2,128,4,128]{4,2,1,3,0:T(8,128)(2,1)} %copy.162), channel_id=1, source_target_pairs={{0,508},{4,0},{8,4},{12,8},{16,12},{20,16},{24,20},{28,24},{32,28}... | collective-permute-start | bytes 1572872 | tf_op jit(solution)/shard_map/ppermute | solution.py:15
  34.5 24.3 %collective-permute-start.5 = (bf16[2,2,128,4,128]{4,2,1,3,0:T(8,128)(2,1)}, bf16[2,2,128,4,128]{4,2,1,3,0:T(8,128)(2,1)}, u32[]{:S(2)}, u32[]{:S(2)}) collective-permute-start(bf16[2,2,128,4,128]{4,2,1,3,0:T(8,128)(2,1)} %copy.162), channel_id=1, source_target_pairs={{0,500},{4,504},{8,508},{12,0},{16,4},{20,8},{24,12},{28,16},{32,2... | collective-permute-start | bytes 1572872 | tf_op jit(solution)/shard_map/ppermute | solution.py:15
  46.6 23.4 %collective-permute-start.3 = (bf16[2,2,128,4,128]{4,2,1,3,0:T(8,128)(2,1)}, bf16[2,2,128,4,128]{4,2,1,3,0:T(8,128)(2,1)S(1)}, u32[]{:S(2)}, u32[]{:S(2)}) collective-permute-start(bf16[2,2,128,4,128]{4,2,1,3,0:T(8,128)(2,1)} %copy.162), channel_id=1, source_target_pairs={{0,504},{4,508},{8,0},{12,4},{16,8},{20,12},{24,16},{28,20},{32,24... | collective-permute-start | bytes 1572872 | tf_op jit(solution)/shard_map/ppermute | solution.py:15
  53.7 6.4 copy-start.18
  53.7 21.5 %copy-start.17 = (pred[2,128]{1,0:T(4,128)(4,1)}, pred[2,128]{1,0:T(4,128)(4,1)S(1)}, u32[]{:S(2)}) copy-start(pred[2,128]{1,0:T(4,128)(4,1)S(1)} %get-tuple-element.24) | copy-start | bytes 772
  60.1 12.6 %copy-start.13 = (f32[2,64,4]{1,0,2:T(2,128)}, f32[2,64,4]{1,0,2:T(2,128)S(1)}, u32[]{:S(2)}) copy-start(f32[2,64,4]{1,0,2:T(2,128)S(1)} %get-tuple-element.37) | copy-start | bytes 6148
  70.0 2.6 copy-start.10
  71.2 1.5 copy-start.14
  85.8 61.6 %copy-start.2 = (bf16[64,2048]{1,0:T(8,128)(2,1)S(1)}, bf16[64,2048]{1,0:T(8,128)(2,1)}, u32[]{:S(2)}) copy-start(bf16[64,2048]{1,0:T(8,128)(2,1)} %param.14) | copy-start | bytes 786436
  88.3 61.0 %copy-start.15 = (f32[2048]{0:T(1024)S(1)}, f32[2048]{0:T(1024)}, u32[]{:S(2)}) copy-start(f32[2048]{0:T(1024)} %param.22) | copy-start | bytes 24580
  90.0 61.3 %copy-start.9 = (bf16[64,512]{1,0:T(8,128)(2,1)}, bf16[64,512]{1,0:T(8,128)(2,1)S(1)}, u32[]{:S(2)}) copy-start(bf16[64,512]{1,0:T(8,128)(2,1)S(1)} %copy_bitcast_fusion) | copy-start | bytes 196612
  537.4 10.8 %copy-start.8 = (bf16[2,2048,128]{2,1,0:T(8,128)(2,1)S(1)}, bf16[2,2048,128]{2,1,0:T(8,128)(2,1)}, u32[]{:S(2)}) copy-start(bf16[2,2048,128]{2,1,0:T(8,128)(2,1)} %param.24) | copy-start | bytes 3145732
  548.2 4.7 copy-start.4
  575.3 14.5 %copy-start.20 = (s32[8]{0:T(128)S(1)}, s32[8]{0:T(128)}, u32[]{:S(2)}) copy-start(s32[8]{0:T(128)} %param.27) | copy-start | bytes 100
  575.3 14.6 %copy-start.3 = (bf16[64,2048]{1,0:T(8,128)(2,1)S(1)}, bf16[64,2048]{1,0:T(8,128)(2,1)}, u32[]{:S(2)}) copy-start(bf16[64,2048]{1,0:T(8,128)(2,1)} %all-reduce.2.cloned.1.call-done) | copy-start | bytes 786436
  575.3 14.6 %copy-start.19 = (bf16[2048,64]{0,1:T(8,128)(2,1)S(1)}, bf16[2048,64]{0,1:T(8,128)(2,1)}, u32[]{:S(2)}) copy-start(bf16[2048,64]{0,1:T(8,128)(2,1)} %param.23) | copy-start | bytes 786436
  575.3 14.9 %copy-start.5 = (s32[64,8]{1,0:T(8,128)S(1)}, s32[64,8]{1,0:T(8,128)}, u32[]{:S(2)}) copy-start(s32[64,8]{1,0:T(8,128)} %copy.180) | copy-start | bytes 6148
  575.3 374.4 %all-to-all-start.1 = ((bf16[128,12,2048]{2,1,0:T(8,128)(2,1)}), bf16[128,12,2048]{2,1,0:T(8,128)(2,1)}, u32[]{:S(2)}, u32[]{:S(2)}) async-start(bf16[128,12,2048]{2,1,0:T(8,128)(2,1)} %reshape.368), calls=%async_computation.1 | async-start | bytes 16777216 | tf_op jit(solution)/shard_map/all_to_all | solution.py:35
  589.5 413.8 %reduce-scatter.2.cloned.1.call-start = ((), (), s32[]{:S(2)}) async-start(), calls=%async_computation.4 | async-start | bytes 327680 | tf_op jit(solution)/shard_map/reduce_scatter | solution.py:119
  950.0 11.2 %copy-start.7 = (bf16[2,64,512]{2,1,0:T(8,128)(2,1)S(1)}, bf16[2,64,512]{2,1,0:T(8,128)(2,1)}, u32[]{:S(2)}) copy-start(bf16[2,64,512]{2,1,0:T(8,128)(2,1)} %param.16) | copy-start | bytes 393220
  950.0 55.0 %copy-start.1 = (bf16[512,2048]{1,0:T(8,128)(2,1)S(1)}, bf16[512,2048]{1,0:T(8,128)(2,1)}, u32[]{:S(2)}) copy-start(bf16[512,2048]{1,0:T(8,128)(2,1)} %param.21) | copy-start | bytes 6291460
Sparse Core Ops, SparseCore 0:
  91.4 55.9 all-reduce.1
  961.3 42.0 reduce-scatter.1
where the time goes:
time: 1010 us
  waiting for transfers between devices  466 us (46%)
  blocking collectives  380 us (38%)
  starting transfers between devices  45 us (4%)
  matrix products  43.1 us (4%)
  local copies, waits for them, and re-layouts  41.4 us (4%)
  other arithmetic  21.6 us (2%)
  between operations  14.6 us (1%)
    all_to_all x1, blocking collectives, body(): lax.all_to_all(outgoing, 'req', split_axis=0, concat_axis=0, tiled=True)  380 us
    all_to_all x1, waiting for transfers between devices, finish_expert(): lax.all_to_all(result, 'req', split_axis=0, concat_axis=0, tiled=True)  359 us
    psum x1, waiting for transfers between devices, body(): lax.psum(partial_proj.astype(jnp.bfloat16), 'tp').astype(jnp.float32)  54.9 us
    reduce_scatter x1, waiting for transfers between devices, body(): lax.psum_scatter(moe_part.astype(jnp.bfloat16), 'tp', scatter_dimension=1...  40.9 us
    ppermute x6, starting transfers between devices, passed_along(): lax.ppermute(value, axis, [(i, (i + by) % devices) for i in range(devices)])  30.5 us
  transfers between devices with their start and end apart: 9, of which 5 were waited for; matrix products, arithmetic and copies ran while one was open for 2% of the time, Pallas kernels for 0%

commit v1 on v0

--- a/solution.py
+++ b/solution.py
@@ -86,7 +86,9 @@
     merged = jnp.sum(factor[..., None] * accs, axis=0) / jnp.sum(factor * totals, axis=0)[..., None]
     attended = merged.astype(jnp.bfloat16).reshape(rows, local_heads * HD)
     partial_proj = jnp.dot(attended, out_proj, preferred_element_type=jnp.float32)
-    attn_proj = lax.psum(partial_proj.astype(jnp.bfloat16), "tp").astype(jnp.float32)
+    attn_proj = jnp.sum(lax.all_gather(partial_proj.astype(jnp.bfloat16), "tp"), axis=0).astype(
+        jnp.float32
+    )
     residual = (hidden.astype(jnp.float32) + attn_proj).astype(jnp.bfloat16)
     resf = residual.astype(jnp.float32)
     normed = (

time: 1010 us -> 985 us (0.975)
  waiting for transfers between devices: 466 us -> 440 us
    psum x1 -> x0, waiting for transfers between devices: 54.9 us -> none  [body(): lax.psum(partial_proj.astype(jnp.bfloat16), 'tp').astype(jnp.float32)]
    all_gather x0 -> x1, waiting for transfers between devices: none -> 28.3 us  [body(): lax.all_gather(partial_proj.astype(jnp.bfloat16), 'tp')]
where the time goes in v1:
time: 985 us; the launch traced here: 984 us
  waiting for transfers between devices  440 us (45%)
  blocking collectives  380 us (39%)
  starting transfers between devices  45.1 us (5%)
  matrix products  42.2 us (4%)
  local copies, waits for them, and re-layouts  40.8 us (4%)
  other arithmetic  20.8 us (2%)
  between operations  14.6 us (1%)
    all_to_all x1, blocking collectives, body(): lax.all_to_all(outgoing, 'req', split_axis=0, concat_axis=0, tiled=True)  380 us
    all_to_all x1, waiting for transfers between devices, finish_expert(): lax.all_to_all(result, 'req', split_axis=0, concat_axis=0, tiled=True)  359 us
    reduce_scatter x1, waiting for transfers between devices, body(): lax.psum_scatter(moe_part.astype(jnp.bfloat16), 'tp', scatter_dimension=1...  40.9 us
    ppermute x6, starting transfers between devices, passed_along(): lax.ppermute(value, axis, [(i, (i + by) % devices) for i in range(devices)])  30.5 us
    all_gather x1, waiting for transfers between devices, body(): lax.all_gather(partial_proj.astype(jnp.bfloat16), 'tp')  28.3 us
  transfers between devices with their start and end apart: 9, of which 5 were waited for; matrix products, arithmetic and copies ran while one was open for 2% of the time, Pallas kernels for 0%

profile of v1, /device:TPU:1, one launch (start us, length us, event | category | flops | bytes accessed | tf_op | source)
XLA Modules:
  0.0 983.5 jit_solution(4483033441599959256)
XLA Ops:
  8.7 13.9 %collective-permute-start.4 = (bf16[2,2]{1,0:T(2,128)(2,1)S(1)}, bf16[2,2]{1,0:T(2,128)(2,1)}, u32[]{:S(2)}, u32[]{:S(2)}) collective-permute-start(bf16[2,2]{1,0:T(2,128)(2,1)S(1)} %pad_maximum_fusion), channel_id=1, source_target_pairs={{0,500},{4,504},{8,508},{12,0},{16,4},{20,8},{24,12},{28,16},{32,2... | collective-permute-start | bytes 32 | tf_op jit(solution)/shard_map/ppermute | solution.py:15
  22.6 4.2 collective-permute-start.2
  26.9 3.1 collective-permute-start
  32.0 1.9 collective-permute-start.1
  34.0 4.8 collective-permute-start.5
  40.0 1.8 fusion.77
  45.5 2.6 collective-permute-start.3
  52.5 1.9 select_reduce_fusion.9
  54.4 3.9 collective-permute-done.5
  58.3 1.3 select_reduce_fusion.3
  59.6 1.4 fusion.47
  61.0 8.5 collective-permute-done.3
  70.7 1.4 fusion.45
  72.2 2.5 select_reduce_fusion.7
  74.6 2.7 concatenate.16
  77.4 2.6 fusion.41
  80.6 2.7 concatenate.18
  87.8 1.3 fusion.9
  91.3 28.3 %all-gather.3.cloned.1.call-done = bf16[256,2048]{1,0:T(8,128)(2,1)} async-done(((bf16[64,2048]{1,0:T(8,128)(2,1)}), bf16[256,2048]{1,0:T(8,128)(2,1)}) %all-gather.3.cloned.1.call-update) | async-done | bytes 1048592 | tf_op jit(solution)/shard_map/all_gather | solution.py:89
  119.6 1.4 reduce_sum.127
  123.1 1.8 copy.187
  124.9 4.3 broadcast_in_dim.165
  129.1 379.9 %all_to_all.10 = bf16[128,12,2048]{2,1,0:T(8,128)(2,1)} all-to-all(bf16[128,12,2048]{2,1,0:T(8,128)(2,1)} %bitcast.128), channel_id=1, replica_groups=mesh['req'=128,'tp'=4] {'req'}, dimensions={0} | all-to-all | bytes 12582912 | tf_op jit(solution)/shard_map/all_to_all | solution.py:112
  509.1 10.8 %reshape.367 = bf16[1536,2048]{1,0:T(8,128)(2,1)} reshape(bf16[128,12,2048]{2,1,0:T(8,128)(2,1)} %all_to_all.10) | data formatting | bytes 12582912 | tf_op jit(solution)/shard_map/reshape | solution.py:113
  519.9 4.6 fusion.26
  524.5 11.9 %convolution_convert_fusion = bf16[1536,2048]{1,0:T(8,128)(2,1)} fusion(bf16[128,2048]{1,0:T(8,128)(2,1)S(1)} %copy-done.3, bf16[1536,2048]{1,0:T(8,128)(2,1)} %reshape.367, f32[1536,128]{1,0:T(8,128)S(1)} %fusion.26, bf16[2,2048,128]{2,1,0:T(8,128)(2,1)S(1)} %copy-done.6), kind=kOutput, calls=%fused_computation.1 | convolution fusion | flops 1614938112 | bytes 14417920 | tf_op jit(solution)/shard_map/dot_general | solution.py:31
  536.4 10.6 %reshape.368 = bf16[128,12,2048]{2,1,0:T(8,128)(2,1)} reshape(bf16[1536,2048]{1,0:T(8,128)(2,1)} %convolution_convert_fusion) | data formatting | bytes 12582912 | tf_op jit(solution)/shard_map/reshape | solution.py:33
  547.0 14.3 %all-to-all-start.1 = ((bf16[128,12,2048]{2,1,0:T(8,128)(2,1)}), bf16[128,12,2048]{2,1,0:T(8,128)(2,1)}, u32[]{:S(2)}, u32[]{:S(2)}) async-start(bf16[128,12,2048]{2,1,0:T(8,128)(2,1)} %reshape.368), calls=%async_computation.1 | async-start | bytes 16777216 | tf_op jit(solution)/shard_map/all_to_all | solution.py:35
  562.9 358.5 %all-to-all-done.1 = bf16[128,12,2048]{2,1,0:T(8,128)(2,1)} async-done(((bf16[128,12,2048]{2,1,0:T(8,128)(2,1)}), bf16[128,12,2048]{2,1,0:T(8,128)(2,1)}, u32[]{:S(2)}, u32[]{:S(2)}) %all-to-all-start.1) | async-done | bytes 6291488 | tf_op jit(solution)/shard_map/all_to_all | solution.py:35
  921.7 11.2 %fusion.6 = bf16[64,2048]{1,0:T(8,128)(2,1)} fusion(bf16[64,128,12]{0,1,2:T(8,128)(2,1)S(1)} %bitcast.129, bf16[128,12,2048]{2,1,0:T(8,128)(2,1)} %all-to-all-done.1), kind=kOutput, calls=%fused_computation.8 | convolution fusion | flops 402784256 | bytes 6750208 | tf_op jit(solution)/shard_map/tdc,dcm->tm/dot_general | solution.py:120
  934.2 40.9 %reduce-scatter.2.cloned.1.call-done = bf16[64,512]{1,0:T(8,128)(2,1)} async-done(((bf16[64,2048]{1,0:T(8,128)(2,1)}), bf16[64,512]{1,0:T(8,128)(2,1)}) %reduce-scatter.2.cloned.1.call-update) | async-done | bytes 65552 | tf_op jit(solution)/shard_map/reduce_scatter | solution.py:121
  975.1 1.6 add_convert_fusion.1
  (107 shorter events, 26.6 us)
Async XLA Ops:
  7.2 82.4 %copy-start = (bf16[512,2048]{1,0:T(8,128)(2,1)S(1)}, bf16[512,2048]{1,0:T(8,128)(2,1)}, u32[]{:S(2)}) copy-start(bf16[512,2048]{1,0:T(8,128)(2,1)} %param.21) | copy-start | bytes 6291460
  7.2 34.6 %copy-start.9 = (bf16[64,512]{1,0:T(8,128)(2,1)S(1)}, bf16[64,512]{1,0:T(8,128)(2,1)}, u32[]{:S(2)}) copy-start(bf16[64,512]{1,0:T(8,128)(2,1)} %param.15) | copy-start | bytes 196612
  7.2 36.0 %copy-start.10 = (s32[64,64]{1,0:T(8,128)S(1)}, s32[64,64]{1,0:T(8,128)}, u32[]{:S(2)}) copy-start(s32[64,64]{1,0:T(8,128)} %param.20) | copy-start | bytes 49156
  7.2 36.1 %copy-start.4 = (bf16[2,64,512]{2,1,0:T(8,128)(2,1)S(1)}, bf16[2,64,512]{2,1,0:T(8,128)(2,1)}, u32[]{:S(2)}) copy-start(bf16[2,64,512]{2,1,0:T(8,128)(2,1)} %param.16) | copy-start | bytes 393220
  7.2 112.4 %all-gather.3.cloned.1.call-start = ((), (), s32[]{:S(2)}) async-start(), calls=%async_computation.4 | async-start | bytes 1310720 | tf_op jit(solution)/shard_map/all_gather | solution.py:89
  8.7 36.7 %collective-permute-start.4 = (bf16[2,2]{1,0:T(2,128)(2,1)S(1)}, bf16[2,2]{1,0:T(2,128)(2,1)}, u32[]{:S(2)}, u32[]{:S(2)}) collective-permute-start(bf16[2,2]{1,0:T(2,128)(2,1)S(1)} %pad_maximum_fusion), channel_id=1, source_target_pairs={{0,500},{4,504},{8,508},{12,0},{16,4},{20,8},{24,12},{28,16},{32,2... | collective-permute-start | bytes 32 | tf_op jit(solution)/shard_map/ppermute | solution.py:15
  22.6 26.6 %collective-permute-start.2 = (bf16[2,2]{1,0:T(2,128)(2,1)S(1)}, bf16[2,2]{1,0:T(2,128)(2,1)}, u32[]{:S(2)}, u32[]{:S(2)}) collective-permute-start(bf16[2,2]{1,0:T(2,128)(2,1)S(1)} %pad_maximum_fusion), channel_id=1, source_target_pairs={{0,504},{4,508},{8,0},{12,4},{16,8},{20,12},{24,16},{28,20},{32,24... | collective-permute-start | bytes 32 | tf_op jit(solution)/shard_map/ppermute | solution.py:15
  26.9 23.6 %collective-permute-start = (bf16[2,2]{1,0:T(2,128)(2,1)S(1)}, bf16[2,2]{1,0:T(2,128)(2,1)}, u32[]{:S(2)}, u32[]{:S(2)}) collective-permute-start(bf16[2,2]{1,0:T(2,128)(2,1)S(1)} %pad_maximum_fusion), channel_id=1, source_target_pairs={{0,508},{4,0},{8,4},{12,8},{16,12},{20,16},{24,20},{28,24},{32,28}... | collective-permute-start | bytes 32 | tf_op jit(solution)/shard_map/ppermute | solution.py:15
  32.0 40.1 %collective-permute-start.1 = (bf16[2,2,128,4,128]{4,2,1,3,0:T(8,128)(2,1)}, bf16[2,2,128,4,128]{4,2,1,3,0:T(8,128)(2,1)}, u32[]{:S(2)}, u32[]{:S(2)}) collective-permute-start(bf16[2,2,128,4,128]{4,2,1,3,0:T(8,128)(2,1)} %copy.162), channel_id=1, source_target_pairs={{0,508},{4,0},{8,4},{12,8},{16,12},{20,16},{24,20},{28,24},{32,28}... | collective-permute-start | bytes 1572872 | tf_op jit(solution)/shard_map/ppermute | solution.py:15
  34.0 24.3 %collective-permute-start.5 = (bf16[2,2,128,4,128]{4,2,1,3,0:T(8,128)(2,1)}, bf16[2,2,128,4,128]{4,2,1,3,0:T(8,128)(2,1)}, u32[]{:S(2)}, u32[]{:S(2)}) collective-permute-start(bf16[2,2,128,4,128]{4,2,1,3,0:T(8,128)(2,1)} %copy.162), channel_id=1, source_target_pairs={{0,500},{4,504},{8,508},{12,0},{16,4},{20,8},{24,12},{28,16},{32,2... | collective-permute-start | bytes 1572872 | tf_op jit(solution)/shard_map/ppermute | solution.py:15
  45.5 24.1 %collective-permute-start.3 = (bf16[2,2,128,4,128]{4,2,1,3,0:T(8,128)(2,1)}, bf16[2,2,128,4,128]{4,2,1,3,0:T(8,128)(2,1)S(1)}, u32[]{:S(2)}, u32[]{:S(2)}) collective-permute-start(bf16[2,2,128,4,128]{4,2,1,3,0:T(8,128)(2,1)} %copy.162), channel_id=1, source_target_pairs={{0,504},{4,508},{8,0},{12,4},{16,8},{20,12},{24,16},{28,20},{32,24... | collective-permute-start | bytes 1572872 | tf_op jit(solution)/shard_map/ppermute | solution.py:15
  52.5 7.1 copy-start.16
  52.5 22.2 %copy-start.15 = (pred[2,128]{1,0:T(4,128)(4,1)}, pred[2,128]{1,0:T(4,128)(4,1)S(1)}, u32[]{:S(2)}) copy-start(pred[2,128]{1,0:T(4,128)(4,1)S(1)} %get-tuple-element.24) | copy-start | bytes 772
  59.6 12.6 %copy-start.11 = (f32[2,64,4]{1,0,2:T(2,128)}, f32[2,64,4]{1,0,2:T(2,128)S(1)}, u32[]{:S(2)}) copy-start(f32[2,64,4]{1,0,2:T(2,128)S(1)} %get-tuple-element.37) | copy-start | bytes 6148
  69.5 2.6 copy-start.8
  70.7 1.5 copy-start.12
  85.3 5.5 copy-start.14
  87.8 33.3 %copy-start.2 = (bf16[64,2048]{1,0:T(8,128)(2,1)S(1)}, bf16[64,2048]{1,0:T(8,128)(2,1)}, u32[]{:S(2)}) copy-start(bf16[64,2048]{1,0:T(8,128)(2,1)} %param.14) | copy-start | bytes 786436
  89.4 32.6 %copy-start.13 = (f32[2048]{0:T(1024)S(1)}, f32[2048]{0:T(1024)}, u32[]{:S(2)}) copy-start(f32[2048]{0:T(1024)} %param.22) | copy-start | bytes 24580
  89.5 33.5 %copy-start.7 = (bf16[64,512]{1,0:T(8,128)(2,1)}, bf16[64,512]{1,0:T(8,128)(2,1)S(1)}, u32[]{:S(2)}) copy-start(bf16[64,512]{1,0:T(8,128)(2,1)S(1)} %copy_bitcast_fusion) | copy-start | bytes 196612
  509.1 10.8 %copy-start.6 = (bf16[2,2048,128]{2,1,0:T(8,128)(2,1)S(1)}, bf16[2,2048,128]{2,1,0:T(8,128)(2,1)}, u32[]{:S(2)}) copy-start(bf16[2,2048,128]{2,1,0:T(8,128)(2,1)} %param.24) | copy-start | bytes 3145732
  519.9 4.6 copy-start.3
  547.0 14.6 %copy-start.18 = (s32[8]{0:T(128)S(1)}, s32[8]{0:T(128)}, u32[]{:S(2)}) copy-start(s32[8]{0:T(128)} %param.27) | copy-start | bytes 100
  547.0 14.6 %copy-start.17 = (bf16[2048,64]{0,1:T(8,128)(2,1)S(1)}, bf16[2048,64]{0,1:T(8,128)(2,1)}, u32[]{:S(2)}) copy-start(bf16[2048,64]{0,1:T(8,128)(2,1)} %param.23) | copy-start | bytes 786436
  547.0 374.4 %all-to-all-start.1 = ((bf16[128,12,2048]{2,1,0:T(8,128)(2,1)}), bf16[128,12,2048]{2,1,0:T(8,128)(2,1)}, u32[]{:S(2)}, u32[]{:S(2)}) async-start(bf16[128,12,2048]{2,1,0:T(8,128)(2,1)} %reshape.368), calls=%async_computation.1 | async-start | bytes 16777216 | tf_op jit(solution)/shard_map/all_to_all | solution.py:35
  561.3 413.8 %reduce-scatter.2.cloned.1.call-start = ((), (), s32[]{:S(2)}) async-start(), calls=%async_computation.3 | async-start | bytes 327680 | tf_op jit(solution)/shard_map/reduce_scatter | solution.py:121
  921.7 11.2 %copy-start.5 = (bf16[2,64,512]{2,1,0:T(8,128)(2,1)S(1)}, bf16[2,64,512]{2,1,0:T(8,128)(2,1)}, u32[]{:S(2)}) copy-start(bf16[2,64,512]{2,1,0:T(8,128)(2,1)} %param.16) | copy-start | bytes 393220
  921.7 55.0 %copy-start.1 = (bf16[512,2048]{1,0:T(8,128)(2,1)S(1)}, bf16[512,2048]{1,0:T(8,128)(2,1)}, u32[]{:S(2)}) copy-start(bf16[512,2048]{1,0:T(8,128)(2,1)} %param.21) | copy-start | bytes 6291460
Sparse Core Ops, SparseCore 0:
  90.9 28.6 all-gather.2
  933.0 42.0 reduce-scatter.1
